TPU v7x, 32 devices: a whole 2x2x4 slice. The times are simulated.
32 devices in a mesh: seq: 16 (over z, y, x), tp: 2 (over core).
Axes of the slice: x: 2, y: 2, z: 4, core: 2. Of those that a mesh axis runs over, the one named last changes fastest.
Arguments:
- mamba_x: bfloat16 [1024, 8192], P('seq', 'tp'), may hold values from -6 to 6
- gate_z: bfloat16 [1024, 8192], P('seq', 'tp'), may hold values from -6 to 6
- b_in: bfloat16 [1024, 1024], P('seq', 'tp'), may hold values from -1.25 to 1.25
- c_in: bfloat16 [1024, 1024], P('seq', 'tp'), may hold values from -1.25 to 1.25
- dt_raw: float32 [128, 1024], P('tp', 'seq'), may hold values from -2 to 6144
- a_log: float32 [128], P('tp'), may hold values from -14 to -3
- skip_d: float32 [128], P('tp'), may hold values from 0.5 to 1.5
- norm_gain: float32 [8192], P('tp'), may hold values from 0.5 to 1.5
- value_weight: bfloat16 [8192, 1024], P('tp'), may hold values from -0.09375 to 0.09375
- queries: bfloat16 [1024, 4096], P('seq', 'tp'), may hold values from -18 to 18
- keys: bfloat16 [1024, 1024], P('seq', 'tp'), may hold values from -4.5 to 4.5
Outputs:
- mamba_out: bfloat16 [1024, 8192], P('seq', 'tp')
- attention: bfloat16 [1024, 4096], P('seq', 'tp')
All inputs are finite; a program needn't handle non-finite values.
Results may differ from a plain program's by a relative error of at most 0.02.
Values may be sent and summed in bfloat16 or wider, within the bound.
A program may use at most 128 MiB of HBM per device.

v0:
```python
import math

import jax
import jax.numpy as jnp
from jax import lax
from jax.sharding import PartitionSpec as P

MHEAD_DIM = 64
STATE = 128
QHEADS = 32
KVHEADS = 8
HEAD_DIM = 128


highest = lax.Precision.HIGHEST
norm_eps = 1e-05


def carried_in(part, axis, combine, identity):
    place = lax.axis_index(axis)
    gathered = jax.tree.map(lambda a: lax.all_gather(a, axis), part)
    state = jax.tree.map(lambda a, e: jnp.zeros_like(a) + jnp.asarray(e, a.dtype), part, identity)

    def one(lap, state):
        return combine(
            state, jax.tree.map(lambda a: lax.dynamic_index_in_dim(a, lap, 0, False), gathered)
        )

    return lax.fori_loop(0, place, one, state)


def block_scan(inputs, b_group, c_group, time_step, decay_rate):
    token_count = inputs.shape[0]
    log_decay = jnp.cumsum(-time_step * decay_rate[..., None], axis=2)
    log_gaps = log_decay[..., :, None] - log_decay[..., None, :]
    causal = jnp.arange(token_count)[:, None] >= jnp.arange(token_count)[None, :]
    decay_mat = jnp.exp(jnp.where(causal, log_gaps, -jnp.inf))
    cross_terms = jnp.einsum("tgn,sgn->gts", c_group, b_group, precision=highest)
    mixing = cross_terms[:, None] * decay_mat * time_step[:, :, None, :]
    local_out = jnp.einsum("gkts,sgkp->tgkp", mixing, inputs, precision=highest)
    tail_weight = jnp.exp(log_decay[..., -1:] - log_decay) * time_step
    summary = jnp.einsum("gks,sgkp,sgn->gkpn", tail_weight, inputs, b_group, precision=highest)
    return (log_decay, local_out, summary, jnp.exp(log_decay[..., -1]))


def carried_out(c_group, state_in, log_decay):
    carried_term = jnp.einsum("tgn,gkpn->tgkp", c_group, state_in, precision=highest)
    return carried_term * jnp.transpose(jnp.exp(log_decay), (2, 0, 1))[..., None]


def gated_norm(ssm_out, gate_z, norm_gain, group_count):
    token_count = ssm_out.shape[0]
    gated = ssm_out * jax.nn.silu(gate_z.astype(jnp.float32))
    grouped = gated.reshape(token_count, group_count, -1)
    inverse = lax.rsqrt(jnp.mean(grouped * grouped, axis=2, keepdims=True) + norm_eps)
    return ((grouped * inverse).reshape(token_count, -1) * norm_gain).astype(jnp.bfloat16)


def chain_combine(earlier, latter):
    return (earlier[0] * latter[0], latter[0][..., None, None] * earlier[1] + latter[1])


def query_layout(payload, kv_here, per_kv):
    count_rows = payload.shape[0]
    shaped = payload.reshape(count_rows, kv_here, per_kv, HEAD_DIM)
    return jnp.transpose(shaped, (1, 2, 0, 3)).reshape(kv_here, per_kv * count_rows, HEAD_DIM)


def row_positions(first_pos, count_rows, per_kv):
    return jnp.tile(first_pos + jnp.arange(count_rows, dtype=jnp.int32), per_kv)


def set_output(finished_set, kv_here, per_kv):
    running_max, running_sum, running_out = finished_set
    count_rows = running_sum.shape[1] // per_kv
    result = (running_out / running_sum[..., None]).astype(jnp.bfloat16)
    result = result.reshape(kv_here, per_kv, count_rows, HEAD_DIM)
    return jnp.transpose(result, (2, 0, 1, 3)).reshape(count_rows, kv_here * per_kv * HEAD_DIM)


def attend(running, query_set, key_slab, value_slab, key_first):
    query_block, query_pos = query_set
    score_scale = 1.0 / math.sqrt(HEAD_DIM)
    key_pos = key_first + jnp.arange(key_slab.shape[1], dtype=jnp.int32)

    def update(current):
        running_max, running_sum, running_out = current
        scores = (
            jnp.einsum("hrd,hcd->hrc", query_block, key_slab, preferred_element_type=jnp.float32)
            * score_scale
        )
        allowed = key_pos[None, :] <= query_pos[:, None]
        scores = jnp.where(allowed[None], scores, -jnp.inf)
        new_max = jnp.maximum(running_max, jnp.max(scores, axis=2))
        weights = jnp.exp(scores - new_max[..., None])
        shrink = jnp.exp(running_max - new_max)
        new_sum = running_sum * shrink + jnp.sum(weights, axis=2)
        new_out = running_out * shrink[..., None] + jnp.einsum(
            "hrc,hcd->hrd",
            weights.astype(jnp.bfloat16),
            value_slab,
            preferred_element_type=jnp.float32,
        )
        return (new_max, new_sum, new_out)

    def unchanged(current):
        return current

    return lax.cond(key_first <= jnp.max(query_pos), update, unchanged, running)


def per_device(
    mamba_x, gate_z, b_in, c_in, dt_raw, a_log, skip_d, norm_gain, value_weight, queries, keys
):
    tokens_here = mamba_x.shape[0]
    group_count = b_in.shape[1] // STATE
    head_count = dt_raw.shape[0]
    per_group = head_count // group_count
    inputs = mamba_x.astype(jnp.float32).reshape(tokens_here, group_count, per_group, MHEAD_DIM)
    b_group = b_in.astype(jnp.float32).reshape(tokens_here, group_count, STATE)
    c_group = c_in.astype(jnp.float32).reshape(tokens_here, group_count, STATE)
    time_step = jax.nn.softplus(dt_raw).reshape(group_count, per_group, tokens_here)
    decay_rate = jnp.exp(a_log).reshape(group_count, per_group)
    log_decay, local_out, summary, totals = block_scan(
        inputs, b_group, c_group, time_step, decay_rate
    )
    _, state_in = carried_in(
        (totals, summary), "seq", chain_combine, (jnp.ones_like(totals), jnp.zeros_like(summary))
    )
    skip_heads = skip_d.reshape(group_count, per_group)[None, :, :, None]
    ssm_out = local_out + carried_out(c_group, state_in, log_decay) + skip_heads * inputs
    mamba_out = gated_norm(ssm_out.reshape(tokens_here, -1), gate_z, norm_gain, group_count)
    kv_here = keys.shape[1] // HEAD_DIM
    per_kv = QHEADS // KVHEADS
    product = jnp.dot(mamba_out, value_weight, preferred_element_type=jnp.float32)
    values = lax.psum_scatter(
        jnp.transpose(
            product.reshape(tokens_here, lax.axis_size("tp") * kv_here, HEAD_DIM), (1, 0, 2)
        ).astype(jnp.bfloat16),
        "tp",
        scatter_dimension=0,
        tiled=True,
    )
    key_heads = jnp.transpose(keys.reshape(tokens_here, kv_here, HEAD_DIM), (1, 0, 2))
    my_index = lax.axis_index("seq")
    query_sets = [
        (
            query_layout(queries, kv_here, per_kv),
            row_positions(my_index * tokens_here, tokens_here, per_kv),
        )
    ]
    initial = tuple(
        (
            (
                jnp.full((kv_here, query_set[0].shape[1]), -jnp.inf, jnp.float32),
                jnp.zeros((kv_here, query_set[0].shape[1]), jnp.float32),
                jnp.zeros((kv_here, query_set[0].shape[1], HEAD_DIM), jnp.float32),
            )
            for query_set in query_sets
        )
    )
    key_portion = lax.all_gather(key_heads, "seq", axis=1, tiled=True)
    value_portion = lax.all_gather(values, "seq", axis=1, tiled=True)
    length = key_portion.shape[1]
    block_len = length
    for multiple in (1, 2, 4):
        block_len = multiple * tokens_here

    def one_block(block_index, current):
        offset = block_index * block_len
        key_slab = lax.dynamic_slice_in_dim(key_portion, offset, block_len, 1)
        value_slab = lax.dynamic_slice_in_dim(value_portion, offset, block_len, 1)
        return tuple(
            (
                attend(current[set_index], query_sets[set_index], key_slab, value_slab, offset)
                for set_index in range(len(query_sets))
            )
        )

    finished = lax.fori_loop(0, length // block_len, one_block, initial)
    outputs = [set_output(finished_set, kv_here, per_kv) for finished_set in finished]
    attention = outputs[0]
    return (mamba_out, attention)


def solution(mesh):
    placed = (
        P("seq", "tp"),
        P("seq", "tp"),
        P("seq", "tp"),
        P("seq", "tp"),
        P("tp", "seq"),
        P("tp"),
        P("tp"),
        P("tp"),
        P("tp", None),
        P("seq", "tp"),
        P("seq", "tp"),
    )
    return jax.shard_map(
        per_device,
        mesh=mesh,
        in_specs=placed,
        out_specs=(P("seq", "tp"), P("seq", "tp")),
        check_vma=False,
    )
```

profile of v0, /device:TPU:24, one launch (start us, length us, event | category | flops | bytes accessed | tf_op | source)
XLA Modules:
  0.0 556.6 jit_solution(8197354195631345208)
XLA Ops:
  10.0 2.1 reshape.113
  12.9 3.7 fusion.12
  16.9 11.5 %copy.107 = bf16[1024,4096]{1,0:T(8,128)(2,1)} copy(bf16[1024,4096]{0,1:T(8,128)(2,1)} %bitcast.69) | data formatting | bytes 16777216 | tf_op jit(solution)/shard_map/dot_general | solution.py:135
  28.4 34.1 %all-gather = f32[64,16,1]{1,2,0:T(1,128)S(1)} all-gather(f32[4,16,1]{1,2,0:T(1,128)S(1)} %bitcast.83), channel_id=2, replica_groups=mesh['seq'=16,'tp'=2] {'seq'}, dimensions={0}, use_global_device_ids=true | all-gather | bytes 4352 | tf_op jit(solution)/shard_map/all_gather | solution.py:21
  62.7 3.2 fusion.15
  65.9 301.0 %all-gather.10.cloned.1.call-done = f32[64,16,64,128]{3,2,1,0:T(8,128)} async-done(((f32[4,16,64,128]{3,2,1,0:T(8,128)}), f32[64,16,64,128]{3,2,1,0:T(8,128)}) %all-gather.10.cloned.1.call-update) | async-done | bytes 33554448 | tf_op jit(solution)/shard_map/all_gather | solution.py:21
  367.2 24.5 %while.32 = (s32[]{:T(128)}, f32[4,16,64,128]{3,2,1,0:T(8,128)S(1)}, s32[]{:T(128)}, f32[16,4,16]{2,1,0:T(4,128)S(1)}, f32[16,4,16,64,128]{4,3,2,1,0:T(8,128)}, /*index=5*/s32[]{:T(128)}, s32[]{:T(128)}, s32[]{:T(128)}) while((s32[]{:T(128)}, f32[4,16,64,128]{3,2,1,0:T(8,128)S(1)}, s32[]{:T(128)}, f32[16,4,16]{2,1,0:T(4,128)S(1)}, ...), condition=%wide.region_2.3_spmd, body=%wide.region_1.2_spmd.sunk | while | flops 1048581 | bytes 6292351 | solution.py:29
  367.2 2.0 bitcast_add_fusion.2
  369.2 2.0 bitcast_add_fusion.2
  371.2 2.0 bitcast_add_fusion.2
  373.3 2.0 bitcast_add_fusion.2
  375.3 2.0 bitcast_add_fusion.2
  377.3 2.0 bitcast_add_fusion.2
  379.3 2.0 bitcast_add_fusion.2
  381.4 2.0 bitcast_add_fusion.2
  383.4 2.0 bitcast_add_fusion.2
  385.4 2.0 bitcast_add_fusion.2
  387.4 2.0 bitcast_add_fusion.2
  389.4 2.0 bitcast_add_fusion.2
  391.6 4.8 fusion.13
  401.9 6.9 %fusion.21 = bf16[8,64,128]{2,1,0:T(8,128)(2,1)} fusion(bf16[8,128,4096]{2,1,0:T(8,128)(2,1)} %bitcast.67, bf16[64,4096]{1,0:T(8,128)(2,1)S(1)} %multiply_convert_fusion), kind=kOutput, calls=%fused_computation.34 | convolution fusion | flops 536936448 | bytes 9043968 | tf_op jit(solution)/shard_map/dot_general | solution.py:135
  409.6 13.2 %reduce-scatter.2.cloned.1.call-done = bf16[4,64,128]{2,1,0:T(8,128)(2,1)} async-done(((bf16[8,64,128]{2,1,0:T(8,128)(2,1)}), bf16[4,64,128]{2,1,0:T(8,128)(2,1)}) %reduce-scatter.2.cloned.1.call-update) | async-done | bytes 65552 | tf_op jit(solution)/shard_map/reduce_scatter | solution.py:136
  423.7 56.9 %all-gather.6.cloned.1.call-done = bf16[4,1024,128]{2,0,1:T(4,128)(2,1)} async-done(((bf16[4,64,128]{2,0,1:T(4,128)(2,1)}), bf16[4,1024,128]{2,0,1:T(4,128)(2,1)}) %all-gather.6.cloned.1.call-update) | async-done | bytes 1048592 | tf_op jit(solution)/shard_map/all_gather | solution.py:162
  482.0 55.2 %all-gather.8.cloned.1.call-done = bf16[4,1024,128]{2,1,0:T(8,128)(2,1)} async-done(((bf16[4,64,128]{2,1,0:T(8,128)(2,1)}), bf16[4,1024,128]{2,1,0:T(8,128)(2,1)}) %all-gather.8.cloned.1.call-update) | async-done | bytes 1048592 | tf_op jit(solution)/shard_map/all_gather | solution.py:163
  537.2 11.5 %while.33 = (s32[]{:T(128)}, f32[4,256]{1,0:T(4,128)S(1)}, f32[4,256]{1,0:T(4,128)S(1)}, f32[4,256,128]{2,1,0:T(8,128)S(1)}, s32[]{:T(128)}, /*index=5*/bf16[4,1...) while((s32[]{:T(128)}, f32[4,256]{1,0:T(4,128)S(1)}, ...), condition=%wide.region_11.12_spmd.clone, body=%wide.region_6.11_spmd.clone.sunk | while | flops 136382720 | bytes 5186101 | solution.py:180
  537.9 2.2 conditional.3
  538.7 1.4 convolution_add_fusion
  540.8 2.2 conditional.3
  543.6 2.2 conditional.3
  544.4 1.4 convolution_add_fusion
  546.5 2.2 conditional.3
  547.3 1.4 convolution_add_fusion
  (113 shorter events, 18.3 us)
Async XLA Ops:
  7.2 359.7 %all-gather.10.cloned.1.call-start = ((), (), s32[]{:S(2)}) async-start(), calls=%async_computation.4 | async-start | bytes 35651584 | tf_op jit(solution)/shard_map/all_gather | solution.py:21
  12.9 3.8 copy-start.4
  12.9 3.8 copy-start.7
  16.7 406.1 %reduce-scatter.2.cloned.1.call-start = ((), (), s32[]{:S(2)}) async-start(), calls=%async_computation.2 | async-start | bytes 196608 | tf_op jit(solution)/shard_map/reduce_scatter | solution.py:136
  16.9 45.7 %copy-start.3 = (bf16[64,512]{1,0:T(8,128)(2,1)S(1)}, bf16[64,512]{1,0:T(8,128)(2,1)}, u32[]{:S(2)}) copy-start(bf16[64,512]{1,0:T(8,128)(2,1)} %param.19) | copy-start | bytes 196612
  400.4 1.1 copy-start
  400.4 1.1 copy-start.6
  401.9 7.0 %copy-start.1 = (bf16[64,4096]{1,0:T(8,128)(2,1)}, bf16[64,4096]{1,0:T(8,128)(2,1)S(1)}, u32[]{:S(2)}) copy-start(bf16[64,4096]{1,0:T(8,128)(2,1)S(1)} %multiply_convert_fusion) | copy-start | bytes 1572868
  401.9 7.0 %copy-start.5 = (bf16[64,512]{1,0:T(8,128)(2,1)S(1)}, bf16[64,512]{1,0:T(8,128)(2,1)}, u32[]{:S(2)}) copy-start(bf16[64,512]{1,0:T(8,128)(2,1)} %param.27) | copy-start | bytes 196612
  401.9 20.9 %copy-start.2 = (bf16[64,2048]{1,0:T(8,128)(2,1)S(1)}, bf16[64,2048]{1,0:T(8,128)(2,1)}, u32[]{:S(2)}) copy-start(bf16[64,2048]{1,0:T(8,128)(2,1)} %param.26) | copy-start | bytes 786436
  408.9 71.8 %all-gather.6.cloned.1.call-start = ((), (), s32[]{:S(2)}) async-start(), calls=%async_computation.1 | async-start | bytes 1114112 | tf_op jit(solution)/shard_map/all_gather | solution.py:162
  409.6 127.6 %all-gather.8.cloned.1.call-start = ((), (), s32[]{:S(2)}) async-start(), calls=%async_computation.3 | async-start | bytes 1114112 | tf_op jit(solution)/shard_map/all_gather | solution.py:163
Sparse Core Ops, SparseCore 0:
  16.8 350.0 all-gather.9
  409.0 13.7 reduce-scatter.1
  425.6 55.0 all-gather.5
  483.2 53.8 all-gather.7
where the time goes:
time: 558 us; the launch traced here: 557 us
  waiting for transfers between devices  426 us (76%)
  blocking collectives  34.1 us (6%)
  other arithmetic  29.5 us (5%)
  matrix products  25.8 us (5%)
  local copies, waits for them, and re-layouts  23 us (4%)
  between operations  14.1 us (3%)
    all_gather x1, waiting for transfers between devices, carried_in(): gathered = jax.tree.map(lambda a: lax.all_gather(a, axis), part)  301 us
    all_gather x1, waiting for transfers between devices, per_device(): key_portion = lax.all_gather(key_heads, 'seq', axis=1, tiled=True)  56.9 us
    all_gather x1, waiting for transfers between devices, per_device(): value_portion = lax.all_gather(values, 'seq', axis=1, tiled=True)  55.2 us
    all_gather x1, blocking collectives, carried_in(): gathered = jax.tree.map(lambda a: lax.all_gather(a, axis), part)  34.1 us
    add x12, other arithmetic, chain_combine(): latter[0][..., None, None] * earlier[1] + latter[1]  23.7 us
    reduce_scatter x1, waiting for transfers between devices, per_device(): lax.psum_scatter(jnp.transpose(product.reshape(tokens_here, lax.axis_size...  13.2 us
    dot_general x1, local copies, waits for them, and re-layouts, per_device(): jnp.dot(mamba_out, value_weight, preferred_element_type=jnp.float32)  11.5 us
  transfers between devices with their start and end apart: 4, of which 4 were waited for; matrix products, arithmetic and copies ran while one was open for 3% of the time, Pallas kernels for 0%

commit v1 on v0

v1 whole, which is shorter than its diff:
```python
import functools
import math

import jax
import jax.numpy as jnp
from jax import lax
from jax.experimental import pallas as pl
from jax.experimental.pallas import tpu as pltpu
from jax.sharding import PartitionSpec as P

MHEAD_DIM = 64
STATE = 128
GROUP_HEADS = 16
QHEADS = 32
KVHEADS = 8
HEAD_DIM = 128
PLANE = 4
BLOCK = 128
NORM_EPS = 1e-05

MESH = pl.DeviceIdType.MESH
HIGHEST = lax.Precision.HIGHEST
f32 = jnp.float32
bf16 = jnp.bfloat16


def dot(a, b, ca=1, cb=0, precision=None):
    return lax.dot_general(
        a, b, (((ca,), (cb,)), ((), ())), precision=precision, preferred_element_type=f32
    )


def kernel(
    n_seq, n_tp,
    x_ref, z_ref, b_ref, c_ref, dt_ref, alog_ref, skip_ref, gain_ref, w_hbm, q_ref, k_ref,
    mo_ref, att_ref,
    w_ref, xo, bo, co, dto, qo, ko, vo, sin, sout, yo, yh, part, vp, scores, probs, sums, ao, loc, scale_out,
    w_sem, own_sem, a_send, a_recv, k_send, k_recv, c_send, c_recv, y_send, y_recv,
    p_send, p_recv, v_send, v_recv, o_send, o_recv,
):
    tok, chans = x_ref.shape
    lanes = chans // PLANE
    heads = lanes // MHEAD_DIM
    nz = n_seq // PLANE
    span = PLANE * tok
    kv_here = k_ref.shape[1] // HEAD_DIM
    q_lanes = q_ref.shape[1] // PLANE
    q_heads = q_lanes // HEAD_DIM
    groups = b_ref.shape[1] // STATE
    seq = lax.axis_index("seq")
    t = lax.axis_index("tp")
    z = seq // PLANE
    p = seq % PLANE

    def seq_id(zz, pp):
        return zz * PLANE + pp

    def cols(index, width):
        return pl.ds(pl.multiple_of(index * width, width), width)

    load_w = pltpu.make_async_copy(w_hbm, w_ref, w_sem)
    load_w.start()

    barrier = pltpu.get_barrier_semaphore()
    for dt_ in range(n_tp):
        for dp in range(PLANE):
            if dt_ or dp:
                pl.semaphore_signal(
                    barrier, inc=1,
                    device_id=(seq_id(z, (p + dp) % PLANE), (t + dt_) % n_tp), device_id_type=MESH,
                )
    for dz in range(1, nz):
        pl.semaphore_signal(
            barrier, inc=1, device_id=(seq_id((z + dz) % nz, p), t), device_id_type=MESH
        )
    pl.semaphore_wait(barrier, n_tp * PLANE - 1 + nz - 1)

    def pieces(to, slot):
        group = to * groups // PLANE
        kv = to * kv_here // PLANE
        return (
            (x_ref.at[:, cols(to, lanes)], xo.at[slot]),
            (b_ref.at[:, cols(group, STATE)], bo.at[slot]),
            (dt_ref.at[to], dto.at[slot]),
            (c_ref.at[:, cols(group, STATE)], co.at[slot]),
            (k_ref.at[:, cols(kv, HEAD_DIM)], ko.at[z, slot]),
            (q_ref.at[:, cols(to, q_lanes)], qo.at[slot]),
        )

    def exchange(d, i, src, dst):
        return pltpu.make_async_remote_copy(
            src_ref=src, dst_ref=dst, send_sem=a_send.at[i, d], recv_sem=a_recv.at[i, d],
            device_id=(seq_id(z, (p + d) % PLANE), t), device_id_type=MESH,
        )

    sends = {}
    for i in range(6):
        for d in range(1, PLANE):
            src, dst = pieces((p + d) % PLANE, p)[i]
            sends[i, d] = exchange(d, i, src, dst)
            sends[i, d].start()
        src, dst = pieces(p, p)[i]
        sends[i, 0] = pltpu.make_async_copy(src, dst, own_sem.at[i])
        sends[i, 0].start()

    def arrived(i):
        for d in range(1, PLANE):
            src, dst = pieces(p, (p + PLANE - d) % PLANE)[i]
            exchange(d, i, src, dst).wait_recv()
        sends[i, 0].wait()

    for i in range(4):
        arrived(i)

    rate = jnp.exp(alog_ref[p])
    spread = (
        lax.broadcasted_iota(jnp.int32, (heads, lanes), 1) // MHEAD_DIM
        == lax.broadcasted_iota(jnp.int32, (heads, lanes), 0)
    ).astype(f32)
    row = lax.broadcasted_iota(jnp.int32, (tok, BLOCK), 0)
    col = lax.broadcasted_iota(jnp.int32, (tok, BLOCK), 1)
    causal = (
        lax.broadcasted_iota(jnp.int32, (BLOCK, BLOCK), 0)
        >= lax.broadcasted_iota(jnp.int32, (BLOCK, BLOCK), 1)
    )
    left_half = lax.broadcasted_iota(jnp.int32, (BLOCK, BLOCK), 1) < MHEAD_DIM
    per_block = BLOCK // tok
    n_blocks = span // BLOCK
    decay_in, added = [], []
    factors = []
    for blk in range(n_blocks):
        l_row = l_col = t_row = t_col = 0.0
        for j in range(per_block):
            raw = dto[blk * per_block + j]
            step = jnp.maximum(raw, 0.0) + jnp.log1p(jnp.exp(-jnp.abs(raw)))
            log_step = -step * rate
            upto = (row + j * tok <= col).astype(f32)
            same = (row + j * tok == col).astype(f32)
            l_row += dot(log_step, upto, precision=HIGHEST)
            l_col += dot(upto, log_step, 0, 1, precision=HIGHEST)
            t_row += dot(step, same, precision=HIGHEST)
            t_col += dot(same, step, 0, 1, precision=HIGHEST)
        tail = jnp.exp(l_col[BLOCK - 1 :, :] - l_col) * t_col
        grown = dot(jnp.exp(l_col), spread, precision=HIGHEST)
        scale_out[blk] = grown
        xb = xo[pl.ds(blk * per_block, per_block)].reshape(BLOCK, lanes)
        bb = bo[pl.ds(blk * per_block, per_block)].reshape(BLOCK, STATE)
        weighted = (xb.astype(f32) * dot(tail, spread, precision=HIGHEST)).astype(bf16)
        added.append(dot(bb, weighted, 0, 0))
        decay_in.append(grown[BLOCK - 1 :, :])
        factors.append((l_row, l_col, t_row, xb, bb))
    before = [(jnp.ones((1, lanes), f32), jnp.zeros((STATE, lanes), f32))]
    for blk in range(n_blocks):
        dec, own = before[-1]
        before.append((dec * decay_in[blk], decay_in[blk] * own + added[blk]))
    plane_dec, plane_own = before[-1]

    n_chunks, _, width = sin.shape

    def chain(i, src, dst):
        return pltpu.make_async_remote_copy(
            src_ref=src, dst_ref=dst, send_sem=c_send.at[i], recv_sem=c_recv.at[i],
            device_id=(seq_id((z + 1) % nz, p), t), device_id_type=MESH,
        )

    @pl.when(z == 0)
    def _():
        sin[...] = jnp.zeros_like(sin)
        for i in range(n_chunks):
            sout[i] = plane_own[:, i * width : (i + 1) * width]
            chain(i, sout.at[i], sin.at[i]).start()

    for blk in range(n_blocks):
        l_row, l_col, t_row, xb, bb = factors[blk]
        cb = co[pl.ds(blk * per_block, per_block)].reshape(BLOCK, STATE)
        cross = dot(cb, bb, 1, 1)
        for pair in range(heads // 2):
            mixes = []
            for h in (2 * pair, 2 * pair + 1):
                gaps = jnp.where(causal, l_col[:, h : h + 1] - l_row[h : h + 1, :], -jnp.inf)
                mixes.append((cross * jnp.exp(gaps) * t_row[h : h + 1, :]).astype(bf16))
            both = dot(jnp.concatenate(mixes, axis=0), xb[:, pair * BLOCK : (pair + 1) * BLOCK])
            loc[blk, :, pair * BLOCK : (pair + 1) * BLOCK] = jnp.where(
                left_half, both[:BLOCK], both[BLOCK:]
            )

    @pl.when(z > 0)
    def _():
        for i in range(n_chunks):
            chain(i, sout.at[i], sin.at[i]).wait_recv()

            @pl.when(z < nz - 1)
            def _():
                part_cols = slice(i * width, (i + 1) * width)
                sout[i] = plane_dec[:, part_cols] * sin[i] + plane_own[:, part_cols]
                chain(i, sout.at[i], sin.at[i]).start()

    skip = dot(jnp.broadcast_to(skip_ref[p], (8, heads)), spread, precision=HIGHEST)[:1]
    for blk in range(n_blocks):
        cb = co[pl.ds(blk * per_block, per_block)].reshape(BLOCK, STATE)
        dec, own = before[blk]
        for i in range(n_chunks):
            pc = slice(i * width, (i + 1) * width)
            state = dec[:, pc] * sin[i] + own[:, pc]
            high = state.astype(bf16)
            low = (state - high.astype(f32)).astype(bf16)
            y = (
                loc[blk, :, pc]
                + scale_out[blk, :, pc] * (dot(cb, high) + dot(cb, low))
                + skip[:, pc] * factors[blk][3][:, pc].astype(f32)
            )
            yo[pl.ds(blk * per_block, per_block), :, pc] = y.astype(bf16).reshape(
                per_block, tok, width
            )

    def give_back(d):
        return pltpu.make_async_remote_copy(
            src_ref=yo.at[(p + d) % PLANE], dst_ref=yh.at[p],
            send_sem=y_send.at[d], recv_sem=y_recv.at[d],
            device_id=(seq_id(z, (p + d) % PLANE), t), device_id_type=MESH,
        )

    for d in range(1, PLANE):
        give_back(d).start()
    yh[p] = yo[p]

    arrived(4)
    arrived(5)

    def later(buffer, zz, send, recv):
        return pltpu.make_async_remote_copy(
            src_ref=buffer.at[z], dst_ref=buffer.at[z], send_sem=send.at[zz], recv_sem=recv.at[z],
            device_id=(seq_id(zz, p), t), device_id_type=MESH,
        )

    def earlier(buffer, zz, send, recv):
        return pltpu.make_async_remote_copy(
            src_ref=buffer.at[zz], dst_ref=buffer.at[zz], send_sem=send.at[zz], recv_sem=recv.at[zz],
            device_id=(seq_id(zz, p), t), device_id_type=MESH,
        )

    def push(buffer, send, recv):
        for zz in range(1, nz):
            @pl.when(zz > z)
            def _():
                later(buffer, zz, send, recv).start()

    def pushed(buffer, send, recv):
        for zz in range(1, nz):
            @pl.when(zz > z)
            def _():
                later(buffer, zz, send, recv).wait_send()

    def take(buffer, send, recv):
        for zz in range(nz - 1):
            @pl.when(zz < z)
            def _():
                earlier(buffer, zz, send, recv).wait_recv()

    push(ko, k_send, k_recv)
    take(ko, k_send, k_recv)
    within = (
        lax.broadcasted_iota(jnp.int32, (span, span), 0)
        >= lax.broadcasted_iota(jnp.int32, (span, span), 1)
    )
    score_scale = 1.0 / math.sqrt(HEAD_DIM)
    for h in range(q_heads):
        query = qo[:, :, h * HEAD_DIM : (h + 1) * HEAD_DIM].reshape(span, HEAD_DIM)
        own_scores = jnp.where(
            within, dot(query, ko[z].reshape(span, HEAD_DIM), 1, 1) * score_scale, -jnp.inf
        )

        def score(zz, largest):
            s = dot(query, ko[zz].reshape(span, HEAD_DIM), 1, 1) * score_scale
            scores[zz] = s
            return jnp.maximum(largest, jnp.max(s, axis=1, keepdims=True))

        largest = lax.fori_loop(0, z, score, jnp.max(own_scores, axis=1, keepdims=True))
        weights = jnp.exp(own_scores - largest)
        probs[z, h] = weights.astype(bf16)

        def weigh(zz, total):
            e = jnp.exp(scores[zz] - largest)
            probs[zz, h] = e.astype(bf16)
            return total + jnp.sum(e, axis=1, keepdims=True)

        total = lax.fori_loop(0, z, weigh, jnp.sum(weights, axis=1, keepdims=True))
        sums[h] = jnp.broadcast_to(total, (span, HEAD_DIM))

    for d in range(1, PLANE):
        give_back(d).wait_recv()
    group_lanes = chans // groups
    for g in range(groups):
        gc = slice(g * group_lanes, (g + 1) * group_lanes)
        if group_lanes == lanes:
            ssm = yh[g].astype(f32)
        else:
            ssm = jnp.concatenate([yh[j].astype(f32) for j in range(PLANE)], axis=1)
        zg = z_ref[:, gc].astype(f32)
        gated = ssm * (zg / (1.0 + jnp.exp(-zg)))
        inverse = lax.rsqrt(jnp.mean(gated * gated, axis=1, keepdims=True) + NORM_EPS)
        mo_ref[:, gc] = (gated * inverse * gain_ref[:, gc]).astype(bf16)
    load_w.wait()
    for n in range(w_ref.shape[1] // 256):
        product = dot(mo_ref[...], w_ref[:, n * 256 : (n + 1) * 256]).astype(bf16)
        part[2 * n] = product[:, :HEAD_DIM]
        part[2 * n + 1] = product[:, HEAD_DIM:]

    def partial_copy(dt_, dp):
        tt, pp = (t + dt_) % n_tp, (p + dp) % PLANE
        return pltpu.make_async_remote_copy(
            src_ref=part.at[tt * kv_here + pp * kv_here // PLANE], dst_ref=vp.at[t, p],
            send_sem=p_send.at[dt_, dp], recv_sem=p_recv.at[dt_, dp],
            device_id=(seq_id(z, pp), tt), device_id_type=MESH,
        )

    offsets = [(dt_, dp) for dt_ in range(n_tp) for dp in range(PLANE) if dt_ or dp]
    for dt_, dp in offsets:
        partial_copy(dt_, dp).start()
    vp[t, p] = part[t * kv_here + p * kv_here // PLANE]
    for dt_, dp in offsets:
        partial_copy(dt_, dp).wait_recv()
    values = vp[0].astype(f32)
    for tt in range(1, n_tp):
        values = values + vp[tt].astype(f32)
    vo[z] = values.astype(bf16)
    push(vo, v_send, v_recv)
    outs = [
        dot(probs[z, h], vo[z].reshape(span, HEAD_DIM)) for h in range(q_heads)
    ]
    take(vo, v_send, v_recv)
    for h in range(q_heads):
        def gather(zz, acc):
            return acc + dot(probs[zz, h], vo[zz].reshape(span, HEAD_DIM))

        acc = lax.fori_loop(0, z, gather, outs[h])
        ao[:, :, h * HEAD_DIM : (h + 1) * HEAD_DIM] = (
            (acc / sums[h]).astype(bf16).reshape(PLANE, tok, HEAD_DIM)
        )

    def hand_out(d):
        return pltpu.make_async_remote_copy(
            src_ref=ao.at[(p + d) % PLANE], dst_ref=att_ref.at[:, cols(p, q_lanes)],
            send_sem=o_send.at[d], recv_sem=o_recv.at[d],
            device_id=(seq_id(z, (p + d) % PLANE), t), device_id_type=MESH,
        )

    for d in range(1, PLANE):
        hand_out(d).start()
    att_ref[:, cols(p, q_lanes)] = ao[p]

    for i in range(6):
        for d in range(1, PLANE):
            sends[i, d].wait_send()
    @pl.when(z < nz - 1)
    def _():
        for i in range(n_chunks):
            chain(i, sout.at[i], sin.at[i]).wait_send()
    for d in range(1, PLANE):
        give_back(d).wait_send()
    pushed(ko, k_send, k_recv)
    pushed(vo, v_send, v_recv)
    for dt_, dp in offsets:
        partial_copy(dt_, dp).wait_send()
    for d in range(1, PLANE):
        hand_out(d).wait_recv()
        hand_out(d).wait_send()


def per_device(
    n_seq, n_tp,
    mamba_x, gate_z, b_in, c_in, dt_raw, a_log, skip_d, norm_gain, value_weight, queries, keys,
):
    tok, chans = mamba_x.shape
    lanes = chans // PLANE
    heads = lanes // MHEAD_DIM
    nz = n_seq // PLANE
    span = PLANE * tok
    q_lanes = queries.shape[1] // PLANE
    q_heads = q_lanes // HEAD_DIM
    width = min(128, lanes)
    n_chunks = lanes // width
    vmem = pl.BlockSpec(memory_space=pltpu.VMEM)
    dma = pltpu.SemaphoreType.DMA
    return pl.pallas_call(
        functools.partial(kernel, n_seq, n_tp),
        out_shape=(
            jax.ShapeDtypeStruct((tok, chans), bf16),
            jax.ShapeDtypeStruct(queries.shape, bf16),
        ),
        in_specs=[vmem] * 8 + [pl.BlockSpec(memory_space=pl.ANY)] + [vmem] * 2,
        out_specs=(vmem, vmem),
        scratch_shapes=[
            pltpu.VMEM(value_weight.shape, bf16),
            pltpu.VMEM((PLANE, tok, lanes), bf16),
            pltpu.VMEM((PLANE, tok, STATE), bf16),
            pltpu.VMEM((PLANE, tok, STATE), bf16),
            pltpu.VMEM((PLANE, heads, tok), f32),
            pltpu.VMEM((PLANE, tok, q_lanes), bf16),
            pltpu.VMEM((nz, PLANE, tok, HEAD_DIM), bf16),
            pltpu.VMEM((nz, PLANE, tok, HEAD_DIM), bf16),
            pltpu.VMEM((n_chunks, STATE, width), f32),
            pltpu.VMEM((n_chunks, STATE, width), f32),
            pltpu.VMEM((PLANE, tok, lanes), bf16),
            pltpu.VMEM((PLANE, tok, lanes), bf16),
            pltpu.VMEM((KVHEADS, tok, HEAD_DIM), bf16),
            pltpu.VMEM((n_tp, PLANE, tok, HEAD_DIM), bf16),
            pltpu.VMEM((nz, span, span), f32),
            pltpu.VMEM((nz, q_heads, span, span), bf16),
            pltpu.VMEM((q_heads, span, HEAD_DIM), f32),
            pltpu.VMEM((PLANE, tok, q_lanes), bf16),
            pltpu.VMEM((span // BLOCK, BLOCK, lanes), f32),
            pltpu.VMEM((span // BLOCK, BLOCK, lanes), f32),
            dma, dma((6,)),
            dma((6, PLANE)), dma((6, PLANE)),
            dma((nz,)), dma((nz,)),
            dma((n_chunks,)), dma((n_chunks,)),
            dma((PLANE,)), dma((PLANE,)),
            dma((n_tp, PLANE)), dma((n_tp, PLANE)),
            dma((nz,)), dma((nz,)),
            dma((PLANE,)), dma((PLANE,)),
        ],
        compiler_params=pltpu.CompilerParams(
            collective_id=0, has_side_effects=True, vmem_limit_bytes=52 * 1024 * 1024
        ),
    )(
        mamba_x, gate_z, b_in, c_in,
        dt_raw.reshape(PLANE, heads, tok), a_log.reshape(PLANE, heads, 1),
        skip_d.reshape(PLANE, 1, heads), norm_gain.reshape(1, chans), value_weight, queries, keys,
    )


def solution(mesh):
    placed = (
        P("seq", "tp"),
        P("seq", "tp"),
        P("seq", "tp"),
        P("seq", "tp"),
        P("tp", "seq"),
        P("tp"),
        P("tp"),
        P("tp"),
        P("tp", None),
        P("seq", "tp"),
        P("seq", "tp"),
    )
    return jax.shard_map(
        functools.partial(per_device, mesh.shape["seq"], mesh.shape["tp"]),
        mesh=mesh,
        in_specs=placed,
        out_specs=(P("seq", "tp"), P("seq", "tp")),
        check_vma=False,
    )
```

time: 558 us -> 73.3 us (0.13)
  waiting for transfers between devices: 426 us -> 0 us
  Pallas kernels: 0 us -> 63.1 us
  blocking collectives: 34.1 us -> 0 us
  other arithmetic: 29.5 us -> 0 us
  matrix products: 25.8 us -> 0 us
  local copies, waits for them, and re-layouts: 23 us -> 9 us
  between operations: 14.1 us -> 0.66 us
    all_gather x3 -> x0, waiting for transfers between devices: 413 us -> none  [the longest x1 301 us: carried_in(): gathered = jax.tree.map(lambda a: lax.all_gather(a, axis), part)]
    pallas_call x0 -> x1, Pallas kernels: none -> 63.1 us  [per_device(): pl.pallas_call(functools.partial(kernel, n_seq, n_tp), out_shape=(jax.Sha...]
    all_gather x1 -> x0, blocking collectives: 34.1 us -> none  [carried_in(): gathered = jax.tree.map(lambda a: lax.all_gather(a, axis), part)]
    dot_general x13 -> x0, matrix products: 25.8 us -> none  [the longest x1 6.91 us: per_device(): jnp.dot(mamba_out, value_weight, preferred_element_type=jnp.float32)]
    add x21 -> x0, other arithmetic: 23.8 us -> none  [the longest x12 23.7 us: chain_combine(): latter[0][..., None, None] * earlier[1] + latter[1]]
    reduce_scatter x1 -> x0, waiting for transfers between devices: 13.2 us -> none  [per_device(): lax.psum_scatter(jnp.transpose(product.reshape(tokens_here, lax.axis_size...]
    dot_general x1 -> x0, local copies, waits for them, and re-layouts: 11.5 us -> none  [per_device(): jnp.dot(mamba_out, value_weight, preferred_element_type=jnp.float32)]
  transfers between devices with their start and end apart: 4 -> 0, of which waited for: 4 -> 0; matrix products, arithmetic and copies ran while one was open for 3% -> 0% of each run, Pallas kernels for 0% -> 0%
where the time goes in v1:
time: 73.3 us; the launch traced here: 72.8 us
  Pallas kernels  63.1 us (86%)
  local copies, waits for them, and re-layouts  9 us (12%)
    pallas_call x1, Pallas kernels, per_device(): pl.pallas_call(functools.partial(kernel, n_seq, n_tp), out_shape=(jax.Sha...  63.1 us
    unnamed x16, local copies, waits for them, and re-layouts  7.48 us

profile of v1, /device:TPU:24, one launch (start us, length us, event | category | flops | bytes accessed | tf_op | source)
XLA Modules:
  0.0 72.8 jit_solution(18088804660729174152)
XLA Ops:
  0.6 0.7 %reshape.18 = f32[4,1,16]{2,0,1:T(4,128)S(1)} reshape(f32[64]{0:T(128)} %param.17) | data formatting | bytes 512 | tf_op jit(solution)/shard_map/reshape | solution.py:429
  1.4 0.8 %reshape.20.alog_ref = f32[4,16,1]{2,1,0:T(8,128)S(1)} reshape(f32[64]{0:T(128)} %param.16) | data formatting | bytes 512 | tf_op jit(solution)/shard_map/reshape | solution.py:428
  2.2 0.0 copy-start
  2.2 1.0 %copy-done = bf16[64,4096]{1,0:T(8,128)(2,1)S(1)} copy-done((bf16[64,4096]{1,0:T(8,128)(2,1)S(1)}, bf16[64,4096]{1,0:T(8,128)(2,1)}, u32[]{:S(2)}) %copy-start) | copy-done | bytes 524312
  3.2 0.0 copy-start.1
  3.2 0.9 %copy-done.1 = bf16[64,2048]{1,0:T(8,128)(2,1)S(1)} copy-done((bf16[64,2048]{1,0:T(8,128)(2,1)S(1)}, bf16[64,2048]{1,0:T(8,128)(2,1)}, u32[]{:S(2)}) %copy-start.1) | copy-done | bytes 262168
  4.2 0.0 copy-start.2
  4.2 0.8 %copy-done.2 = bf16[64,512]{1,0:T(8,128)(2,1)S(1)} copy-done((bf16[64,512]{1,0:T(8,128)(2,1)S(1)}, bf16[64,512]{1,0:T(8,128)(2,1)}, u32[]{:S(2)}) %copy-start.2) | copy-done | bytes 65560
  5.0 0.0 copy-start.3
  5.0 0.8 %copy-done.3 = bf16[64,512]{1,0:T(8,128)(2,1)S(1)} copy-done((bf16[64,512]{1,0:T(8,128)(2,1)S(1)}, bf16[64,512]{1,0:T(8,128)(2,1)}, u32[]{:S(2)}) %copy-start.3) | copy-done | bytes 65560
  5.8 0.0 copy-start.4
  5.8 0.8 %copy-done.4 = bf16[64,512]{1,0:T(8,128)(2,1)S(1)} copy-done((bf16[64,512]{1,0:T(8,128)(2,1)S(1)}, bf16[64,512]{1,0:T(8,128)(2,1)}, u32[]{:S(2)}) %copy-start.4) | copy-done | bytes 65560
  6.7 0.0 copy-start.5
  6.7 0.8 %copy-done.5 = f32[64,64]{1,0:T(8,128)S(1)} copy-done((f32[64,64]{1,0:T(8,128)S(1)}, f32[64,64]{1,0:T(8,128)}, u32[]{:S(2)}) %copy-start.5) | copy-done | bytes 16408
  7.4 0.0 copy-start.6
  7.4 0.7 copy-done.6
  8.2 63.1 %shard_map.122 = (bf16[64,4096]{1,0:T(8,128)(2,1)S(1)}, bf16[64,2048]{1,0:T(8,128)(2,1)S(1)}) custom-call(bf16[64,4096]{1,0:T(8,128)(2,1)S(1)} %copy-done, bf16[64,4096]{1,0:T(8,128)(2,1)} %z_ref.1, bf16[64,512]{1,0:T(8,128)(2,1)S(1)} %copy-done.2, bf16[64,512]{1,0:T(8,128)(2,1)S(1)} %copy-done.3, f32[4,16,64]{2,1,0:T(8,128)S(1)} %bitcast.3, ...), custom_call_target="tpu_custom_call" | custom-call | tf_op jit(solution)/shard_map/pallas_call | solution.py:385
  71.3 0.8 %copy.17 = bf16[64,4096]{1,0:T(8,128)(2,1)} copy(bf16[64,4096]{1,0:T(8,128)(2,1)S(1)} %get-tuple-element.4) | data formatting | bytes 1048576
  72.1 0.7 copy.18
Async XLA Ops:
  2.2 1.0 %copy-start = (bf16[64,4096]{1,0:T(8,128)(2,1)S(1)}, bf16[64,4096]{1,0:T(8,128)(2,1)}, u32[]{:S(2)}) copy-start(bf16[64,4096]{1,0:T(8,128)(2,1)} %x_ref.1) | copy-start | bytes 1572868
  3.2 0.9 %copy-start.1 = (bf16[64,2048]{1,0:T(8,128)(2,1)S(1)}, bf16[64,2048]{1,0:T(8,128)(2,1)}, u32[]{:S(2)}) copy-start(bf16[64,2048]{1,0:T(8,128)(2,1)} %q_ref.1) | copy-start | bytes 786436
  4.2 0.8 %copy-start.2 = (bf16[64,512]{1,0:T(8,128)(2,1)S(1)}, bf16[64,512]{1,0:T(8,128)(2,1)}, u32[]{:S(2)}) copy-start(bf16[64,512]{1,0:T(8,128)(2,1)} %b_ref.1) | copy-start | bytes 196612
  5.0 0.8 %copy-start.3 = (bf16[64,512]{1,0:T(8,128)(2,1)S(1)}, bf16[64,512]{1,0:T(8,128)(2,1)}, u32[]{:S(2)}) copy-start(bf16[64,512]{1,0:T(8,128)(2,1)} %c_ref.1) | copy-start | bytes 196612
  5.8 0.8 %copy-start.4 = (bf16[64,512]{1,0:T(8,128)(2,1)S(1)}, bf16[64,512]{1,0:T(8,128)(2,1)}, u32[]{:S(2)}) copy-start(bf16[64,512]{1,0:T(8,128)(2,1)} %k_ref.1) | copy-start | bytes 196612
  6.7 0.8 %copy-start.5 = (f32[64,64]{1,0:T(8,128)S(1)}, f32[64,64]{1,0:T(8,128)}, u32[]{:S(2)}) copy-start(f32[64,64]{1,0:T(8,128)} %param.15) | copy-start | bytes 49156
  7.4 0.7 copy-start.6

commit v2 on v1

v2 whole, which is shorter than its diff:
```python
import functools
import math

import jax
import jax.numpy as jnp
from jax import lax
from jax.experimental import pallas as pl
from jax.experimental.pallas import tpu as pltpu
from jax.sharding import PartitionSpec as P

MHEAD_DIM = 64
STATE = 128
GROUP_HEADS = 16
QHEADS = 32
KVHEADS = 8
HEAD_DIM = 128
PLANE = 4
BLOCK = 128
NORM_EPS = 1e-05

MESH = pl.DeviceIdType.MESH
f32 = jnp.float32
bf16 = jnp.bfloat16


def dot(a, b, ca=1, cb=0):
    return lax.dot_general(a, b, (((ca,), (cb,)), ((), ())), preferred_element_type=f32)


def kernel(
    n_seq, n_tp,
    x_hbm, z_hbm, b_hbm, c_hbm, dt_hbm, alog_ref, skip_ref, gain_ref, w_hbm, q_hbm, k_hbm,
    mo_ref, att_ref,
    w_ref, z_ref, xo, bo, co, dto, qo, ko, vo, sin, sout, yo, yh, part, vp, scores, probs, sums, accs, ao,
    grown, tail_w, silu,
    w_sem, z_sem, own_sem, a_send, a_recv, k_send, k_recv, c_send, c_recv, y_send, y_recv,
    p_send, p_recv, v_send, v_recv, o_send, o_recv,
):
    tok, chans = x_hbm.shape
    lanes = chans // PLANE
    heads = lanes // MHEAD_DIM
    nz = n_seq // PLANE
    span = PLANE * tok
    kv_here = k_hbm.shape[1] // HEAD_DIM
    q_lanes = q_hbm.shape[1] // PLANE
    q_heads = q_lanes // HEAD_DIM
    groups = b_hbm.shape[1] // STATE
    seq = lax.axis_index("seq")
    t = lax.axis_index("tp")
    z = seq // PLANE
    p = seq % PLANE

    def seq_id(zz, pp):
        return zz * PLANE + pp

    def cols(index, width):
        return pl.ds(pl.multiple_of(index * width, width), width)

    barrier = pltpu.get_barrier_semaphore()
    for dt_ in range(n_tp):
        for dp in range(PLANE):
            if dt_ or dp:
                pl.semaphore_signal(
                    barrier, inc=1,
                    device_id=(seq_id(z, (p + dp) % PLANE), (t + dt_) % n_tp), device_id_type=MESH,
                )
    for dz in range(1, nz):
        pl.semaphore_signal(
            barrier, inc=1, device_id=(seq_id((z + dz) % nz, p), t), device_id_type=MESH
        )

    def pieces(to, slot):
        group = to * groups // PLANE
        kv = to * kv_here // PLANE
        return (
            (k_hbm.at[:, cols(kv, HEAD_DIM)], ko.at[z, slot]),
            (dt_hbm.at[to], dto.at[slot]),
            (b_hbm.at[:, cols(group, STATE)], bo.at[slot]),
            (x_hbm.at[:, cols(to, lanes)], xo.at[slot]),
            (c_hbm.at[:, cols(group, STATE)], co.at[slot]),
            (q_hbm.at[:, cols(to, q_lanes)], qo.at[slot]),
        )

    def exchange(d, i, src, dst):
        return pltpu.make_async_remote_copy(
            src_ref=src, dst_ref=dst, send_sem=a_send.at[i, d], recv_sem=a_recv.at[i, d],
            device_id=(seq_id(z, (p + d) % PLANE), t), device_id_type=MESH,
        )

    sends = {}
    for i in range(6):
        src, dst = pieces(p, p)[i]
        sends[i, 0] = pltpu.make_async_copy(src, dst, own_sem.at[i])
        sends[i, 0].start()
    pl.semaphore_wait(barrier, n_tp * PLANE - 1 + nz - 1)
    for i in range(6):
        for d in range(1, PLANE):
            src, dst = pieces((p + d) % PLANE, p)[i]
            sends[i, d] = exchange(d, i, src, dst)
            sends[i, d].start()
    load_z = pltpu.make_async_copy(z_hbm, z_ref, z_sem)
    load_z.start()
    load_w = pltpu.make_async_copy(w_hbm, w_ref, w_sem)
    load_w.start()

    def arrived(i):
        for d in range(1, PLANE):
            src, dst = pieces(p, (p + PLANE - d) % PLANE)[i]
            exchange(d, i, src, dst).wait_recv()
        sends[i, 0].wait()

    def later(buffer, zz, send, recv):
        return pltpu.make_async_remote_copy(
            src_ref=buffer.at[z], dst_ref=buffer.at[z], send_sem=send.at[zz], recv_sem=recv.at[z],
            device_id=(seq_id(zz, p), t), device_id_type=MESH,
        )

    def earlier(buffer, zz, send, recv):
        return pltpu.make_async_remote_copy(
            src_ref=buffer.at[zz], dst_ref=buffer.at[zz], send_sem=send.at[zz], recv_sem=recv.at[zz],
            device_id=(seq_id(zz, p), t), device_id_type=MESH,
        )

    def push(buffer, send, recv):
        for zz in range(1, nz):
            @pl.when(zz > z)
            def _():
                later(buffer, zz, send, recv).start()

    def pushed(buffer, send, recv):
        for zz in range(1, nz):
            @pl.when(zz > z)
            def _():
                later(buffer, zz, send, recv).wait_send()

    arrived(0)
    push(ko, k_send, k_recv)

    arrived(1)
    per_block = BLOCK // tok
    n_blocks = span // BLOCK
    rows = n_blocks * heads
    head_row = lax.broadcasted_iota(jnp.int32, (heads, BLOCK), 0)
    log_rate = jnp.zeros((heads, BLOCK), f32)
    for h in range(heads):
        log_rate = jnp.where(head_row == h, alog_ref[0, p * heads + h], log_rate)
    raw = jnp.concatenate(
        [
            jnp.concatenate([dto[blk * per_block + j] for j in range(per_block)], axis=1)
            for blk in range(n_blocks)
        ],
        axis=0,
    )
    steps = jnp.maximum(raw, 0.0) + jnp.log1p(jnp.exp(-jnp.abs(raw)))
    log_step = -steps * jnp.concatenate([jnp.exp(log_rate)] * n_blocks, axis=0)
    row = lax.broadcasted_iota(jnp.int32, (BLOCK, BLOCK), 0)
    col = lax.broadcasted_iota(jnp.int32, (BLOCK, BLOCK), 1)
    causal = row >= col
    left_half = col < MHEAD_DIM
    upto = (row <= col).astype(bf16)
    first = log_step.astype(bf16).astype(f32)
    second = (log_step - first).astype(bf16).astype(f32)
    third = log_step - first - second
    summed = dot(jnp.concatenate([first, second, third], axis=0).astype(bf16), upto)
    l_rows = summed[:rows] + summed[rows : 2 * rows] + summed[2 * rows :]
    turned = jnp.concatenate([l_rows, steps, jnp.zeros((BLOCK - 2 * rows, BLOCK), f32)], axis=0).T

    def column(kind, blk, h):
        at = kind * rows + blk * heads + h
        return jnp.broadcast_to(turned[:, at : at + 1], (BLOCK, BLOCK))

    n_chunks = sin.shape[0]
    for blk in range(n_blocks):
        for i in range(n_chunks):
            l_both = jnp.where(left_half, column(0, blk, 2 * i), column(0, blk, 2 * i + 1))
            t_both = jnp.where(left_half, column(1, blk, 2 * i), column(1, blk, 2 * i + 1))
            grown[blk, i] = jnp.exp(l_both)
            tail_w[blk, i] = jnp.exp(l_both[BLOCK - 1 :, :] - l_both) * t_both

    def chain(i):
        return pltpu.make_async_remote_copy(
            src_ref=sout.at[i], dst_ref=sin.at[i], send_sem=c_send.at[i], recv_sem=c_recv.at[i],
            device_id=(seq_id((z + 1) % nz, p), t), device_id_type=MESH,
        )

    def chunk(i):
        return slice(i * BLOCK, (i + 1) * BLOCK)

    arrived(2)
    arrived(3)
    b_blocks = [
        bo[pl.ds(blk * per_block, per_block)].reshape(BLOCK, STATE) for blk in range(n_blocks)
    ]

    def x_block(blk, i):
        return xo[pl.ds(blk * per_block, per_block), :, chunk(i)].reshape(BLOCK, BLOCK)

    before = {}
    for i in range(n_chunks):
        dec, own = jnp.ones((1, BLOCK), f32), jnp.zeros((STATE, BLOCK), f32)
        for blk in range(n_blocks):
            before[blk, i] = (dec, own)
            weighted = (x_block(blk, i).astype(f32) * tail_w[blk, i]).astype(bf16)
            fade = grown[blk, i, BLOCK - 1 :, :]
            own = fade * own + dot(b_blocks[blk], weighted, 0, 0)
            dec = dec * fade
        before[n_blocks, i] = (dec, own)
        sout[i] = own

        @pl.when(z == 0)
        def _():
            chain(i).start()

    @pl.when(z == 0)
    def _():
        sin[...] = jnp.zeros_like(sin)

    arrived(4)
    c_blocks = [
        co[pl.ds(blk * per_block, per_block)].reshape(BLOCK, STATE) for blk in range(n_blocks)
    ]
    cross = [dot(c_blocks[blk], b_blocks[blk], 1, 1) for blk in range(n_blocks)]

    def give_back(i, d):
        return pltpu.make_async_remote_copy(
            src_ref=yo.at[i, (p + d) % PLANE], dst_ref=yh.at[i, p],
            send_sem=y_send.at[i, d], recv_sem=y_recv.at[i, d],
            device_id=(seq_id(z, (p + d) % PLANE), t), device_id_type=MESH,
        )

    within = (
        lax.broadcasted_iota(jnp.int32, (span, span), 0)
        >= lax.broadcasted_iota(jnp.int32, (span, span), 1)
    )
    score_scale = 1.0 / math.sqrt(HEAD_DIM)

    def attend(h):
        query = qo[:, :, h * HEAD_DIM : (h + 1) * HEAD_DIM].reshape(span, HEAD_DIM)
        own_scores = jnp.where(
            within, dot(query, ko[z].reshape(span, HEAD_DIM), 1, 1) * score_scale, -jnp.inf
        )

        def score(zz, largest):
            s = dot(query, ko[zz].reshape(span, HEAD_DIM), 1, 1) * score_scale
            scores[zz] = s
            return jnp.maximum(largest, jnp.max(s, axis=1, keepdims=True))

        largest = lax.fori_loop(0, z, score, jnp.max(own_scores, axis=1, keepdims=True))
        weights = jnp.exp(own_scores - largest)
        probs[z, h] = weights.astype(bf16)

        def weigh(zz, total):
            e = jnp.exp(scores[zz] - largest)
            probs[zz, h] = e.astype(bf16)
            return total + jnp.sum(e, axis=1, keepdims=True)

        total = lax.fori_loop(0, z, weigh, jnp.sum(weights, axis=1, keepdims=True))
        sums[h] = jnp.broadcast_to(total, (span, HEAD_DIM))

    attended = 0
    for i in range(n_chunks):
        @pl.when(z > 0)
        def _():
            chain(i).wait_recv()

            @pl.when(z < nz - 1)
            def _():
                dec, own = before[n_blocks, i]
                sout[i] = dec * sin[i] + sout[i]
                chain(i).start()

        skip = jnp.where(
            left_half, skip_ref[0, p * heads + 2 * i], skip_ref[0, p * heads + 2 * i + 1]
        )
        for blk in range(n_blocks):
            mixes = []
            for h in (2 * i, 2 * i + 1):
                at = blk * heads + h
                gaps = jnp.where(causal, column(0, blk, h) - l_rows[at : at + 1, :], -jnp.inf)
                mixes.append((cross[blk] * jnp.exp(gaps) * steps[at : at + 1, :]).astype(bf16))
            xb = x_block(blk, i)
            both = dot(jnp.concatenate(mixes, axis=0), xb)
            local = jnp.where(left_half, both[:BLOCK], both[BLOCK:])
            dec, own = before[blk, i]
            state = dec * sin[i] + own
            high = state.astype(bf16)
            low = (state - high.astype(f32)).astype(bf16)
            carried = dot(c_blocks[blk], high) + dot(c_blocks[blk], low)
            y = local + grown[blk, i] * carried + skip * xb.astype(f32)
            yo[i, pl.ds(blk * per_block, per_block)] = y.astype(bf16).reshape(
                per_block, tok, BLOCK
            )
        for d in range(1, PLANE):
            give_back(i, d).start()
        yh[i, p] = yo[i, p]
        while attended < q_heads and (attended + 1) * n_chunks <= (i + 1) * q_heads:
            if attended == 0:
                arrived(5)
                for zz in range(nz - 1):
                    @pl.when(zz < z)
                    def _():
                        earlier(ko, zz, k_send, k_recv).wait_recv()
            attend(attended)
            attended += 1

    load_z.wait()
    zg = z_ref[...].astype(f32)
    silu[...] = zg / (1.0 + jnp.exp(-zg))
    for i in range(n_chunks):
        for d in range(1, PLANE):
            give_back(i, d).wait_recv()
    group_lanes = chans // groups
    for g in range(groups):
        gc = slice(g * group_lanes, (g + 1) * group_lanes)
        owners = range(g * PLANE // groups, (g + 1) * PLANE // groups)
        ssm = jnp.concatenate([yh[i, j] for j in owners for i in range(n_chunks)], axis=1)
        gated = ssm.astype(f32) * silu[:, gc]
        inverse = lax.rsqrt(jnp.mean(gated * gated, axis=1, keepdims=True) + NORM_EPS)
        mo_ref[:, gc] = (gated * inverse * gain_ref[:, gc]).astype(bf16)

    def partial_copy(dt_, dp):
        tt, pp = (t + dt_) % n_tp, (p + dp) % PLANE
        return pltpu.make_async_remote_copy(
            src_ref=part.at[tt * kv_here + pp * kv_here // PLANE], dst_ref=vp.at[t, p],
            send_sem=p_send.at[dt_, dp], recv_sem=p_recv.at[dt_, dp],
            device_id=(seq_id(z, pp), tt), device_id_type=MESH,
        )

    offsets = [(dt_, dp) for dt_ in range(n_tp) for dp in range(PLANE) if dt_ or dp]
    load_w.wait()
    for n in range(w_ref.shape[1] // 256):
        product = dot(mo_ref[...], w_ref[:, n * 256 : (n + 1) * 256]).astype(bf16)
        part[2 * n] = product[:, :HEAD_DIM]
        part[2 * n + 1] = product[:, HEAD_DIM:]
        for dt_, dp in offsets:
            tt, pp = (t + dt_) % n_tp, (p + dp) % PLANE

            @pl.when((tt * kv_here + pp * kv_here // PLANE) // 2 == n)
            def _():
                partial_copy(dt_, dp).start()

    vp[t, p] = part[t * kv_here + p * kv_here // PLANE]
    accs[...] = jnp.zeros_like(accs)

    def take(zz):
        earlier(vo, zz, v_send, v_recv).wait_recv()
        for h in range(q_heads):
            accs[h] += dot(probs[zz, h], vo[zz].reshape(span, HEAD_DIM))

    for zz in range(nz - 2):
        @pl.when(zz < z - 1)
        def _():
            take(zz)

    for dt_, dp in offsets:
        partial_copy(dt_, dp).wait_recv()
    values = vp[0].astype(f32)
    for tt in range(1, n_tp):
        values = values + vp[tt].astype(f32)
    vo[z] = values.astype(bf16)
    push(vo, v_send, v_recv)

    for zz in range(nz - 1):
        @pl.when(zz == z - 1)
        def _():
            take(zz)

    def hand_out(h, d):
        return pltpu.make_async_remote_copy(
            src_ref=ao.at[h, (p + d) % PLANE], dst_ref=att_ref.at[:, cols(p * q_heads + h, HEAD_DIM)],
            send_sem=o_send.at[h, d], recv_sem=o_recv.at[h, d],
            device_id=(seq_id(z, (p + d) % PLANE), t), device_id_type=MESH,
        )

    for h in range(q_heads):
        acc = accs[h] + dot(probs[z, h], vo[z].reshape(span, HEAD_DIM))
        ao[h] = (acc / sums[h]).astype(bf16).reshape(PLANE, tok, HEAD_DIM)
        for d in range(1, PLANE):
            hand_out(h, d).start()
        att_ref[:, cols(p * q_heads + h, HEAD_DIM)] = ao[h, p]

    for i in range(6):
        for d in range(1, PLANE):
            sends[i, d].wait_send()

    @pl.when(z < nz - 1)
    def _():
        for i in range(n_chunks):
            chain(i).wait_send()

    for i in range(n_chunks):
        for d in range(1, PLANE):
            give_back(i, d).wait_send()
    pushed(ko, k_send, k_recv)
    pushed(vo, v_send, v_recv)
    for dt_, dp in offsets:
        partial_copy(dt_, dp).wait_send()
    for h in range(q_heads):
        for d in range(1, PLANE):
            hand_out(h, d).wait_recv()
            hand_out(h, d).wait_send()


def per_device(
    n_seq, n_tp,
    mamba_x, gate_z, b_in, c_in, dt_raw, a_log, skip_d, norm_gain, value_weight, queries, keys,
):
    tok, chans = mamba_x.shape
    lanes = chans // PLANE
    heads = lanes // MHEAD_DIM
    nz = n_seq // PLANE
    span = PLANE * tok
    q_lanes = queries.shape[1] // PLANE
    q_heads = q_lanes // HEAD_DIM
    n_chunks = lanes // BLOCK
    n_blocks = span // BLOCK
    vmem = pl.BlockSpec(memory_space=pltpu.VMEM)
    smem = pl.BlockSpec(memory_space=pltpu.SMEM)
    hbm = pl.BlockSpec(memory_space=pl.ANY)
    dma = pltpu.SemaphoreType.DMA
    return pl.pallas_call(
        functools.partial(kernel, n_seq, n_tp),
        out_shape=(
            jax.ShapeDtypeStruct((tok, chans), bf16),
            jax.ShapeDtypeStruct(queries.shape, bf16),
        ),
        in_specs=[hbm] * 5 + [smem] * 2 + [vmem] + [hbm] * 3,
        out_specs=(vmem, vmem),
        scratch_shapes=[
            pltpu.VMEM(value_weight.shape, bf16),
            pltpu.VMEM((tok, chans), bf16),
            pltpu.VMEM((PLANE, tok, lanes), bf16),
            pltpu.VMEM((PLANE, tok, STATE), bf16),
            pltpu.VMEM((PLANE, tok, STATE), bf16),
            pltpu.VMEM((PLANE, heads, tok), f32),
            pltpu.VMEM((PLANE, tok, q_lanes), bf16),
            pltpu.VMEM((nz, PLANE, tok, HEAD_DIM), bf16),
            pltpu.VMEM((nz, PLANE, tok, HEAD_DIM), bf16),
            pltpu.VMEM((n_chunks, STATE, BLOCK), f32),
            pltpu.VMEM((n_chunks, STATE, BLOCK), f32),
            pltpu.VMEM((n_chunks, PLANE, tok, BLOCK), bf16),
            pltpu.VMEM((n_chunks, PLANE, tok, BLOCK), bf16),
            pltpu.VMEM((KVHEADS, tok, HEAD_DIM), bf16),
            pltpu.VMEM((n_tp, PLANE, tok, HEAD_DIM), bf16),
            pltpu.VMEM((nz, span, span), f32),
            pltpu.VMEM((nz, q_heads, span, span), bf16),
            pltpu.VMEM((q_heads, span, HEAD_DIM), f32),
            pltpu.VMEM((q_heads, span, HEAD_DIM), f32),
            pltpu.VMEM((q_heads, PLANE, tok, HEAD_DIM), bf16),
            pltpu.VMEM((n_blocks, n_chunks, BLOCK, BLOCK), f32),
            pltpu.VMEM((n_blocks, n_chunks, BLOCK, BLOCK), f32),
            pltpu.VMEM((tok, chans), f32),
            dma, dma, dma((6,)),
            dma((6, PLANE)), dma((6, PLANE)),
            dma((nz,)), dma((nz,)),
            dma((n_chunks,)), dma((n_chunks,)),
            dma((n_chunks, PLANE)), dma((n_chunks, PLANE)),
            dma((n_tp, PLANE)), dma((n_tp, PLANE)),
            dma((nz,)), dma((nz,)),
            dma((q_heads, PLANE)), dma((q_heads, PLANE)),
        ],
        compiler_params=pltpu.CompilerParams(
            collective_id=0, has_side_effects=True, vmem_limit_bytes=52 * 1024 * 1024
        ),
    )(
        mamba_x, gate_z, b_in, c_in,
        dt_raw.reshape(PLANE, heads, tok), a_log.reshape(1, -1),
        skip_d.reshape(1, -1), norm_gain.reshape(1, chans), value_weight, queries, keys,
    )


def solution(mesh):
    placed = (
        P("seq", "tp"),
        P("seq", "tp"),
        P("seq", "tp"),
        P("seq", "tp"),
        P("tp", "seq"),
        P("tp"),
        P("tp"),
        P("tp"),
        P("tp", None),
        P("seq", "tp"),
        P("seq", "tp"),
    )
    return jax.shard_map(
        functools.partial(per_device, mesh.shape["seq"], mesh.shape["tp"]),
        mesh=mesh,
        in_specs=placed,
        out_specs=(P("seq", "tp"), P("seq", "tp")),
        check_vma=False,
    )
```

time: 73.3 us -> 59.2 us (0.81)
  Pallas kernels: 63.1 us -> 48.6 us
    pallas_call x1, Pallas kernels: 63.1 us -> 48.6 us  [per_device(): pl.pallas_call(functools.partial(kernel, n_seq, n_tp), out_shape=(jax.Sha...]
    reshape x2 -> x0, local copies, waits for them, and re-layouts: 1.52 us -> none  [the longest x1 0.78 us: per_device(): a_log.reshape(PLANE, heads, 1)]
    unnamed x16 -> x20, local copies, waits for them, and re-layouts: 7.48 us -> 8.78 us
where the time goes in v2:
time: 59.2 us; the launch traced here: 58.1 us
  Pallas kernels  48.6 us (82%)
  local copies, waits for them, and re-layouts  8.78 us (15%)
  between operations  0.66 us (1%)
    pallas_call x1, Pallas kernels, per_device(): pl.pallas_call(functools.partial(kernel, n_seq, n_tp), out_shape=(jax.Sha...  48.6 us
    unnamed x20, local copies, waits for them, and re-layouts  8.78 us

profile of v2, /device:TPU:24, one launch (start us, length us, event | category | flops | bytes accessed | tf_op | source)
XLA Modules:
  0.0 58.1 jit_solution(9838910062927346641)
XLA Ops:
  0.6 0.0 copy-start
  0.6 1.0 %copy-done = bf16[64,4096]{1,0:T(8,128)(2,1)S(1)} copy-done((bf16[64,4096]{1,0:T(8,128)(2,1)S(1)}, bf16[64,4096]{1,0:T(8,128)(2,1)}, u32[]{:S(2)}) %copy-start) | copy-done | bytes 524312
  1.7 0.0 copy-start.1
  1.7 0.9 %copy-done.1 = bf16[64,2048]{1,0:T(8,128)(2,1)S(1)} copy-done((bf16[64,2048]{1,0:T(8,128)(2,1)S(1)}, bf16[64,2048]{1,0:T(8,128)(2,1)}, u32[]{:S(2)}) %copy-start.1) | copy-done | bytes 262168
  2.6 0.0 copy-start.2
  2.6 0.8 %copy-done.2 = bf16[64,512]{1,0:T(8,128)(2,1)S(1)} copy-done((bf16[64,512]{1,0:T(8,128)(2,1)S(1)}, bf16[64,512]{1,0:T(8,128)(2,1)}, u32[]{:S(2)}) %copy-start.2) | copy-done | bytes 65560
  3.5 0.0 copy-start.3
  3.5 0.8 %copy-done.3 = bf16[64,512]{1,0:T(8,128)(2,1)S(1)} copy-done((bf16[64,512]{1,0:T(8,128)(2,1)S(1)}, bf16[64,512]{1,0:T(8,128)(2,1)}, u32[]{:S(2)}) %copy-start.3) | copy-done | bytes 65560
  4.3 0.0 copy-start.4
  4.3 0.8 %copy-done.4 = bf16[64,512]{1,0:T(8,128)(2,1)S(1)} copy-done((bf16[64,512]{1,0:T(8,128)(2,1)S(1)}, bf16[64,512]{1,0:T(8,128)(2,1)}, u32[]{:S(2)}) %copy-start.4) | copy-done | bytes 65560
  5.1 0.0 copy-start.5
  5.1 0.8 %copy-done.5 = f32[64,64]{1,0:T(8,128)S(1)} copy-done((f32[64,64]{1,0:T(8,128)S(1)}, f32[64,64]{1,0:T(8,128)}, u32[]{:S(2)}) %copy-start.5) | copy-done | bytes 16408
  5.9 0.0 copy-start.6
  5.9 0.7 %copy-done.6 = f32[4096]{0:T(1024)S(1)} copy-done((f32[4096]{0:T(1024)S(1)}, f32[4096]{0:T(1024)}, u32[]{:S(2)}) %copy-start.6) | copy-done | bytes 16408
  6.6 0.0 copy-start.7
  6.6 0.7 %copy-done.7 = f32[64]{0:T(128)S(1)} copy-done((f32[64]{0:T(128)S(1)}, f32[64]{0:T(128)}, u32[]{:S(2)}) %copy-start.7) | copy-done | bytes 280
  7.3 0.0 copy-start.8
  7.3 0.7 %copy-done.8 = f32[64]{0:T(128)S(1)} copy-done((f32[64]{0:T(128)S(1)}, f32[64]{0:T(128)}, u32[]{:S(2)}) %copy-start.8) | copy-done | bytes 280
  7.9 48.6 %shard_map.122 = (bf16[64,4096]{1,0:T(8,128)(2,1)S(1)}, bf16[64,2048]{1,0:T(8,128)(2,1)S(1)}) custom-call(bf16[64,4096]{1,0:T(8,128)(2,1)S(1)} %copy-done, bf16[64,4096]{1,0:T(8,128)(2,1)} %z_hbm.1, bf16[64,512]{1,0:T(8,128)(2,1)S(1)} %copy-done.2, bf16[64,512]{1,0:T(8,128)(2,1)S(1)} %copy-done.3, f32[4,16,64]{2,1,0:T(8,128)S(1)} %bitcast.4, ...), custom_call_target="tpu_custom_call" | custom-call | tf_op jit(solution)/shard_map/pallas_call | solution.py:421
  56.6 0.8 %copy.15 = bf16[64,4096]{1,0:T(8,128)(2,1)} copy(bf16[64,4096]{1,0:T(8,128)(2,1)S(1)} %get-tuple-element.4) | data formatting | bytes 1048576
  57.4 0.7 %copy.16 = bf16[64,2048]{1,0:T(8,128)(2,1)} copy(bf16[64,2048]{1,0:T(8,128)(2,1)S(1)} %get-tuple-element.5) | data formatting | bytes 524288
Async XLA Ops:
  0.6 1.0 %copy-start = (bf16[64,4096]{1,0:T(8,128)(2,1)S(1)}, bf16[64,4096]{1,0:T(8,128)(2,1)}, u32[]{:S(2)}) copy-start(bf16[64,4096]{1,0:T(8,128)(2,1)} %x_hbm.1) | copy-start | bytes 1572868
  1.7 0.9 %copy-start.1 = (bf16[64,2048]{1,0:T(8,128)(2,1)S(1)}, bf16[64,2048]{1,0:T(8,128)(2,1)}, u32[]{:S(2)}) copy-start(bf16[64,2048]{1,0:T(8,128)(2,1)} %q_hbm.1) | copy-start | bytes 786436
  2.6 0.8 %copy-start.2 = (bf16[64,512]{1,0:T(8,128)(2,1)S(1)}, bf16[64,512]{1,0:T(8,128)(2,1)}, u32[]{:S(2)}) copy-start(bf16[64,512]{1,0:T(8,128)(2,1)} %b_hbm.1) | copy-start | bytes 196612
  3.5 0.8 %copy-start.3 = (bf16[64,512]{1,0:T(8,128)(2,1)S(1)}, bf16[64,512]{1,0:T(8,128)(2,1)}, u32[]{:S(2)}) copy-start(bf16[64,512]{1,0:T(8,128)(2,1)} %c_hbm.1) | copy-start | bytes 196612
  4.3 0.8 %copy-start.4 = (bf16[64,512]{1,0:T(8,128)(2,1)S(1)}, bf16[64,512]{1,0:T(8,128)(2,1)}, u32[]{:S(2)}) copy-start(bf16[64,512]{1,0:T(8,128)(2,1)} %k_hbm.1) | copy-start | bytes 196612
  5.1 0.8 %copy-start.5 = (f32[64,64]{1,0:T(8,128)S(1)}, f32[64,64]{1,0:T(8,128)}, u32[]{:S(2)}) copy-start(f32[64,64]{1,0:T(8,128)} %param.15) | copy-start | bytes 49156
  5.9 0.7 %copy-start.6 = (f32[4096]{0:T(1024)S(1)}, f32[4096]{0:T(1024)}, u32[]{:S(2)}) copy-start(f32[4096]{0:T(1024)} %param.18) | copy-start | bytes 49156
  6.6 0.7 %copy-start.7 = (f32[64]{0:T(128)S(1)}, f32[64]{0:T(128)}, u32[]{:S(2)}) copy-start(f32[64]{0:T(128)} %param.16) | copy-start | bytes 772
  7.3 0.7 %copy-start.8 = (f32[64]{0:T(128)S(1)}, f32[64]{0:T(128)}, u32[]{:S(2)}) copy-start(f32[64]{0:T(128)} %param.17) | copy-start | bytes 772
